TPU v7x, 32 devices: a whole 2x2x4 slice. The times are simulated.
32 devices in a mesh: groups: 2 (over y), zone: 4 (over x, core), tile: 4 (over z).
Axes of the slice: x: 2, y: 2, z: 4, core: 2. Of those that a mesh axis runs over, the one named last changes fastest.
Arguments:
- backscatter: bfloat16 [8, 2, 256, 512], P(('groups', 'zone'), None, 'tile'), parts along dimension 0, may hold values from -6 to 6
- row_bank: bfloat16 [16, 128, 128], replicated, may hold values from -0.3125 to 0.3125
- row_index: int32 [8, 4, 3], P(('groups', 'zone')), parts along dimension 0, may hold values from 0 to 3
- row_pick: int32 [8, 4, 3], P(('groups', 'zone')), parts along dimension 0, may hold values from 0 to 15
- row_mask: int32 [8, 4, 3], P(('groups', 'zone')), parts along dimension 0, may hold values 0 or 1
- column_bank: bfloat16 [16, 128, 128], replicated, may hold values from -0.3125 to 0.3125
- column_index: int32 [8, 2, 3], P(('groups', 'zone')), parts along dimension 0, may hold values from 0 to 1
- column_pick: int32 [8, 2, 3], P(('groups', 'zone')), parts along dimension 0, may hold values from 0 to 15
- column_mask: int32 [8, 2, 3], P(('groups', 'zone')), parts along dimension 0, may hold values 0 or 1
Outputs:
- geocoded: bfloat16 [8, 2, 256, 512], P(('groups', 'zone'), None, None, 'tile'), parts along dimension 0
There are 2 independent parts, one for each index of `groups`. A program takes and returns all parts, laid end to end along the dimension named above; an argument that names none is the same for every part. Nothing has to cross between parts.
All inputs are finite; a program needn't handle non-finite values. No bound on the sum of `row_mask` or of `column_mask` on one device may be relied on, other than what follows from the above.
Results may differ from a plain program's by a relative error of at most 0.0049.
Values may be sent and summed in bfloat16 or wider, within the bound.
A program may use at most 64 MiB of HBM per device.

v0:
```python
import jax
import jax.numpy as jnp
from jax import lax
from jax.sharding import PartitionSpec as P

BLOCK = 128
EDGE = 64


def passed_along(block, axis, distance):
    devices = range(lax.axis_size(axis))
    route = [(i - distance, i) for i in devices if i - distance in devices]
    return lax.ppermute(block, axis, route)


def swap_panels(top_panel, bottom_panel):
    from_below = passed_along(top_panel, "zone", -1)
    from_above = passed_along(bottom_panel, "zone", 1)
    zone_index = lax.axis_index("zone")
    last_zone = lax.axis_size("zone") - 1
    feather = ((jnp.arange(EDGE, dtype=jnp.float32) + 0.5) / EDGE)[:, None]
    lower_blend = (
        (1.0 - feather) * bottom_panel.astype(jnp.float32)
        + feather * from_below.astype(jnp.float32)
    ).astype(jnp.bfloat16)
    upper_blend = (
        (1.0 - feather) * from_above.astype(jnp.float32) + feather * top_panel.astype(jnp.float32)
    ).astype(jnp.bfloat16)
    new_bottom = jnp.where(zone_index < last_zone, lower_blend, bottom_panel)
    new_top = jnp.where(zone_index > 0, upper_blend, top_panel)
    return (new_top, new_bottom)


def on_device(
    backscatter,
    row_bank,
    row_index,
    row_pick,
    row_mask,
    column_bank,
    column_index,
    column_pick,
    column_mask,
):
    image = backscatter[0]
    channels, lin_dev, samples = image.shape
    column_blocks = samples // BLOCK
    blocks = image.reshape(channels, lin_dev, column_blocks, BLOCK)
    gathered = blocks[:, :, row_index[0], :]
    row_weights = row_bank[row_pick[0]] * row_mask[0].astype(jnp.bfloat16)[:, :, None, None]
    along_samples = jnp.einsum(
        "clqbi,qbij->clqj", gathered, row_weights, preferred_element_type=jnp.float32
    )
    along_samples = along_samples.astype(jnp.bfloat16).reshape(channels, lin_dev, samples)
    line_blocks = column_index.shape[1]
    rows = line_blocks * BLOCK
    column_weights = (
        column_bank[column_pick[0]] * column_mask[0].astype(jnp.bfloat16)[:, :, None, None]
    )
    band_table = column_index[0]
    every_id = jnp.arange(line_blocks, dtype=jnp.int32)
    moved = lax.all_to_all(along_samples, "tile", split_axis=2, concat_axis=1, tiled=True)
    count = moved.shape[0]
    line_tiles = moved.reshape(count, line_blocks, BLOCK, BLOCK)
    picked = line_tiles[:, band_table[every_id]]
    result = jnp.einsum(
        "crbik,rboi->crok", picked, column_weights[every_id], preferred_element_type=jnp.float32
    )
    result = result.astype(jnp.bfloat16).reshape(count, every_id.shape[0] * BLOCK, BLOCK)
    new_top, new_bottom = swap_panels(result[:, :EDGE], result[:, rows - EDGE :])
    gridded = jnp.concatenate([new_top, result[:, EDGE : rows - EDGE], new_bottom], axis=1)
    return gridded[None]


def solution(mesh):
    in_specs = (
        P(("groups", "zone"), None, "tile", None),
        P(),
        P(("groups", "zone"), None, None),
        P(("groups", "zone"), None, None),
        P(("groups", "zone"), None, None),
        P(),
        P(("groups", "zone"), None, None),
        P(("groups", "zone"), None, None),
        P(("groups", "zone"), None, None),
    )
    out_specs = P(("groups", "zone"), None, None, "tile")
    return jax.shard_map(
        on_device, mesh=mesh, in_specs=in_specs, out_specs=out_specs, check_vma=False
    )
```

profile of v0, /device:TPU:1, one launch (start us, length us, event | category | flops | bytes accessed | tf_op | source)
XLA Modules:
  0.0 29.0 jit_solution(11059921443978826120)
XLA Ops:
  0.0 1.0 %reshape_squeeze.3 = bf16[2,64,4,128]{3,2,1,0:T(4,128)(2,1)S(1)} reshape(bf16[1,2,64,512]{3,2,1,0:T(8,128)(2,1)} %param.9) | data formatting | bytes 262144 | tf_op jit(solution)/shard_map/reshape;squeeze | solution.py:48
  1.0 0.6 %copy-done.2 = s32[1,4,3]{1,0,2:T(1,128)S(1)} copy-done((s32[1,4,3]{1,0,2:T(1,128)S(1)}, s32[1,4,3]{1,0,2:T(1,128)}, u32[]{:S(2)}) %copy-start.2) | copy-done | bytes 72
  1.7 0.1 copy.41
  1.8 0.1 reshape.158
  1.9 0.7 %copy-done.3 = s32[1,4,3]{1,0,2:T(1,128)S(1)} copy-done((s32[1,4,3]{1,0,2:T(1,128)S(1)}, s32[1,4,3]{1,0,2:T(1,128)}, u32[]{:S(2)}) %copy-start.3) | copy-done | bytes 72
  2.6 0.1 copy.39
  2.7 0.1 reshape.150
  2.8 0.7 %copy-done.4 = s32[1,4,3]{1,0,2:T(1,128)S(1)} copy-done((s32[1,4,3]{1,0,2:T(1,128)S(1)}, s32[1,4,3]{1,0,2:T(1,128)}, u32[]{:S(2)}) %copy-start.4) | copy-done | bytes 72
  3.4 0.1 copy.40
  3.5 0.6 %gather_fusion.3 = bf16[12,2,64,128]{3,2,1,0:T(8,128)(2,1)S(1)} fusion(bf16[2,64,4,128]{3,1,2,0:T(8,128)(2,1)S(1)} %copy.42, s32[1024]{0:T(1024)S(1)} %pad_clamp_fusion.1), kind=kCustom, calls=%fused_computation.3 | custom fusion | bytes 786480 | tf_op jit(solution)/shard_map/gather | solution.py:49
  4.2 0.6 %gather_fusion.2 = bf16[12,128,128]{2,1,0:T(8,128)(2,1)S(1)} fusion(bf16[16,128,128]{2,1,0:T(8,128)(2,1)S(1)} %copy-done, s32[1024]{0:T(1024)S(1)} %pad_clamp_fusion.2), kind=kCustom, calls=%fused_computation.2 | custom fusion | bytes 786480 | tf_op jit(solution)/shard_map/gather | solution.py:50
  4.8 0.3 %fusion.2 = bf16[2,64,4,128]{3,1,0,2:T(8,128)(2,1)S(1)} fusion(bf16[2,64,4,3,128]{4,1,0,3,2:T(8,128)(2,1)S(1)} %bitcast.85, bf16[4,3,128,128]{3,2,1,0:T(8,128)(2,1)S(1)} %bitcast.87, bf16[4,3]{1,0:T(4,128)(2,1)S(1)} %bitcast.89), kind=kOutput, calls=%fused_computation.10 | convolution fusion | flops 51183616 | bytes 917528 | tf_op jit(solution)/shard_map/clqbi,qbij->clqj/dot_general | solution.py:51
  5.2 0.2 copy.54
  5.3 0.9 %reshape.188 = bf16[4,2,8192]{2,1,0:T(2,128)(2,1)} reshape(bf16[512,2,64]{2,1,0:T(2,128)(2,1)S(1)} %bitcast.79) | data formatting | bytes 262144
  6.2 5.4 %all-to-all-start = ((bf16[4,2,8192]{2,1,0:T(2,128)(2,1)}), bf16[4,2,8192]{2,1,0:T(2,128)(2,1)S(1)}, u32[]{:S(2)}, u32[]{:S(2)}) async-start(bf16[4,2,8192]{2,1,0:T(2,128)(2,1)} %reshape.188), calls=%async_computation | async-start | bytes 262144 | tf_op jit(solution)/shard_map/all_to_all | solution.py:62
  11.7 0.7 %copy-done.5 = s32[1,2,3]{2,1,0:T(2,128)S(1)} copy-done((s32[1,2,3]{2,1,0:T(2,128)S(1)}, s32[1,2,3]{2,1,0:T(2,128)}, u32[]{:S(2)}) %copy-start.5) | copy-done | bytes 48
  12.3 0.1 reshape.134
  12.4 0.7 %copy-done.6 = s32[1,2,3]{2,1,0:T(2,128)S(1)} copy-done((s32[1,2,3]{2,1,0:T(2,128)S(1)}, s32[1,2,3]{2,1,0:T(2,128)}, u32[]{:S(2)}) %copy-start.6) | copy-done | bytes 48
  13.1 0.7 %copy-done.1 = s32[1,2,3]{2,1,0:T(2,128)S(1)} copy-done((s32[1,2,3]{2,1,0:T(2,128)S(1)}, s32[1,2,3]{2,1,0:T(2,128)}, u32[]{:S(2)}) %copy-start.1) | copy-done | bytes 48
  13.8 0.6 %gather_fusion.4 = s32[2,3]{1,0:T(2,128)S(1)} fusion(s32[2,3]{1,0:T(2,128)S(1)} %bitcast.88, s32[1024]{0:T(1024)S(1)} %pad_clamp_fusion.3), kind=kCustom, calls=%fused_computation.4 | custom fusion | bytes 56 | tf_op jit(solution)/shard_map/gather | solution.py:65
  14.3 1.6 %gather_fusion = bf16[6,128,128]{2,1,0:T(8,128)(2,1)S(1)} fusion(bf16[16,128,128]{2,1,0:T(8,128)(2,1)} %param.14, s32[1024]{0:T(1024)S(1)} %pad_clamp_fusion.4), kind=kCustom, calls=%fused_computation | custom fusion | bytes 393240 | tf_op jit(solution)/shard_map/gather | solution.py:58
  16.0 0.1 broadcast_multiply_fusion
  16.2 0.6 %gather_fusion.1 = bf16[2,3,128,128]{3,2,1,0:T(8,128)(2,1)S(1)} fusion(bf16[2,3,128,128]{3,2,1,0:T(8,128)(2,1)S(1)} %broadcast_multiply_fusion, s32[1024]{0:T(1024)S(1)} %pad_clamp_fusion.3), kind=kCustom, calls=%fused_computation.1 | custom fusion | bytes 393224 | tf_op jit(solution)/shard_map/gather | solution.py:67
  16.8 0.2 reshape.189
  17.0 0.2 copy.55
  17.2 0.6 %gather_fusion.5 = bf16[6,2,128,128]{3,2,1,0:T(8,128)(2,1)S(1)} fusion(bf16[2,2,128,128]{3,2,1,0:T(8,128)(2,1)S(1)} %bitcast.77, s32[1024]{0:T(1024)S(1)} %pad_clamp_fusion), kind=kCustom, calls=%fused_computation.5 | custom fusion | bytes 786456 | tf_op jit(solution)/shard_map/gather | solution.py:65
  17.8 0.2 fusion.3
  18.1 4.9 %collective-permute-start = (bf16[2,64,128]{2,1,0:T(8,128)(2,1)S(1)}, bf16[2,64,128]{2,1,0:T(8,128)(2,1)S(1)}, u32[]{:S(2)}, u32[]{:S(2)}) collective-permute-start(bf16[2,64,128]{2,1,0:T(8,128)(2,1)S(1)} %get-tuple-element.7), channel_id=1, source_target_pairs={{0,4},{4,8},{8,12},{1,5},{5,9},{9,13},{2,6},{6,10},{10,14},{3,7},{... | collective-permute-start | bytes 98312 | tf_op jit(solution)/shard_map/ppermute | solution.py:13
  23.0 1.9 %collective-permute-start.1 = (bf16[2,64,128]{2,1,0:T(8,128)(2,1)S(1)}, bf16[2,64,128]{2,1,0:T(8,128)(2,1)S(1)}, u32[]{:S(2)}, u32[]{:S(2)}) collective-permute-start(bf16[2,64,128]{2,1,0:T(8,128)(2,1)S(1)} %get-tuple-element.8), channel_id=1, source_target_pairs={{4,0},{8,4},{12,8},{5,1},{9,5},{13,9},{6,2},{10,6},{14,10},{7,3},{... | collective-permute-start | bytes 98312 | tf_op jit(solution)/shard_map/ppermute | solution.py:13
  25.0 3.3 %collective-permute-done.1 = bf16[2,64,128]{2,1,0:T(8,128)(2,1)S(1)} collective-permute-done((bf16[2,64,128]{2,1,0:T(8,128)(2,1)S(1)}, bf16[2,64,128]{2,1,0:T(8,128)(2,1)S(1)}, u32[]{:S(2)}, u32[]{:S(2)}) %collective-permute-start.1) | collective-permute-done | bytes 32800 | tf_op jit(solution)/shard_map/ppermute | solution.py:13
  28.3 0.1 fusion.8
  28.4 0.7 %maximum_bitcast_fusion = bf16[1,2,256,128]{3,2,1,0:T(8,128)(2,1)} fusion(bf16[2,64,128]{2,1,0:T(8,128)(2,1)S(1)} %get-tuple-element.6, bf16[2,128,128]{2,1,0:T(8,128)(2,1)S(1)} %slice.26, bf16[2,64,128]{2,1,0:T(8,128)(2,1)S(1)} %get-tuple-element.5), kind=kLoop, calls=%fused_computation.16 | loop fusion | flops 393216 | bytes 262144 | tf_op jit(solution)/shard_map/broadcast_in_dim | solution.py:72
  (29 shorter events, 0.2 us)
Async XLA Ops:
  0.0 4.2 %copy-start = (bf16[16,128,128]{2,1,0:T(8,128)(2,1)S(1)}, bf16[16,128,128]{2,1,0:T(8,128)(2,1)}, u32[]{:S(2)}) copy-start(bf16[16,128,128]{2,1,0:T(8,128)(2,1)} %param.10) | copy-start | bytes 1572868
  1.0 0.7 %copy-start.2 = (s32[1,4,3]{1,0,2:T(1,128)S(1)}, s32[1,4,3]{1,0,2:T(1,128)}, u32[]{:S(2)}) copy-start(s32[1,4,3]{1,0,2:T(1,128)} %param.11) | copy-start | bytes 148
  1.9 0.7 %copy-start.3 = (s32[1,4,3]{1,0,2:T(1,128)S(1)}, s32[1,4,3]{1,0,2:T(1,128)}, u32[]{:S(2)}) copy-start(s32[1,4,3]{1,0,2:T(1,128)} %param.12) | copy-start | bytes 148
  2.7 0.7 %copy-start.4 = (s32[1,4,3]{1,0,2:T(1,128)S(1)}, s32[1,4,3]{1,0,2:T(1,128)}, u32[]{:S(2)}) copy-start(s32[1,4,3]{1,0,2:T(1,128)} %param.13) | copy-start | bytes 148
  6.2 10.5 %all-to-all-start = ((bf16[4,2,8192]{2,1,0:T(2,128)(2,1)}), bf16[4,2,8192]{2,1,0:T(2,128)(2,1)S(1)}, u32[]{:S(2)}, u32[]{:S(2)}) async-start(bf16[4,2,8192]{2,1,0:T(2,128)(2,1)} %reshape.188), calls=%async_computation | async-start | bytes 262144 | tf_op jit(solution)/shard_map/all_to_all | solution.py:62
  11.7 0.7 %copy-start.5 = (s32[1,2,3]{2,1,0:T(2,128)S(1)}, s32[1,2,3]{2,1,0:T(2,128)}, u32[]{:S(2)}) copy-start(s32[1,2,3]{2,1,0:T(2,128)} %param.16) | copy-start | bytes 76
  12.4 0.7 %copy-start.6 = (s32[1,2,3]{2,1,0:T(2,128)S(1)}, s32[1,2,3]{2,1,0:T(2,128)}, u32[]{:S(2)}) copy-start(s32[1,2,3]{2,1,0:T(2,128)} %param.17) | copy-start | bytes 76
  13.1 0.7 %copy-start.1 = (s32[1,2,3]{2,1,0:T(2,128)S(1)}, s32[1,2,3]{2,1,0:T(2,128)}, u32[]{:S(2)}) copy-start(s32[1,2,3]{2,1,0:T(2,128)} %param.15) | copy-start | bytes 76
  18.1 6.9 %collective-permute-start = (bf16[2,64,128]{2,1,0:T(8,128)(2,1)S(1)}, bf16[2,64,128]{2,1,0:T(8,128)(2,1)S(1)}, u32[]{:S(2)}, u32[]{:S(2)}) collective-permute-start(bf16[2,64,128]{2,1,0:T(8,128)(2,1)S(1)} %get-tuple-element.7), channel_id=1, source_target_pairs={{0,4},{4,8},{8,12},{1,5},{5,9},{9,13},{2,6},{6,10},{10,14},{3,7},{... | collective-permute-start | bytes 98312 | tf_op jit(solution)/shard_map/ppermute | solution.py:13
  23.0 5.2 %collective-permute-start.1 = (bf16[2,64,128]{2,1,0:T(8,128)(2,1)S(1)}, bf16[2,64,128]{2,1,0:T(8,128)(2,1)S(1)}, u32[]{:S(2)}, u32[]{:S(2)}) collective-permute-start(bf16[2,64,128]{2,1,0:T(8,128)(2,1)S(1)} %get-tuple-element.8), channel_id=1, source_target_pairs={{4,0},{8,4},{12,8},{5,1},{9,5},{13,9},{6,2},{10,6},{14,10},{7,3},{... | collective-permute-start | bytes 98312 | tf_op jit(solution)/shard_map/ppermute | solution.py:13
where the time goes:
time: 29.5 us; the launch traced here: 29 us
  starting transfers between devices  12.3 us (42%)
  local copies, waits for them, and re-layouts  11.8 us (40%)
  waiting for transfers between devices  3.26 us (11%)
  other arithmetic  0.91 us (3%)
  matrix products  0.57 us (2%)
    ppermute x2, starting transfers between devices, passed_along(): return lax.ppermute(block, axis, route)  6.83 us
    all_to_all x1, starting transfers between devices, on_device(): lax.all_to_all(along_samples, 'tile', split_axis=2, concat_axis=1, tiled=...  5.42 us
    unnamed x16, local copies, waits for them, and re-layouts  5.14 us
    ppermute x2, waiting for transfers between devices, passed_along(): return lax.ppermute(block, axis, route)  3.26 us
    gather x1, local copies, waits for them, and re-layouts, on_device(): column_bank[column_pick[0]]  1.62 us
    gather x2, local copies, waits for them, and re-layouts, on_device(): picked = line_tiles[:, band_table[every_id]]  1.18 us
    another operation x2, local copies, waits for them, and re-layouts, on_device(): blocks = image.reshape(channels, lin_dev, column_blocks, BLOCK)  1.02 us
    broadcast_in_dim x1, other arithmetic, on_device(): return gridded[None]  0.67 us
  transfers between devices with their start and end apart: 3, of which 1 were waited for; matrix products, arithmetic and copies ran while one was open for 11% of the time, Pallas kernels for 0%

commit v1 on v0

v1 whole, which is shorter than its diff:
```python
import functools

import jax
import jax.numpy as jnp
from jax import lax
from jax.experimental import pallas as pl
from jax.experimental.pallas import tpu as pltpu
from jax.sharding import PartitionSpec as P

BLOCK = 128
EDGE = 64
MESH = pl.DeviceIdType.MESH


def repeat(count, body):
    if count <= 8:
        for i in range(count):
            body(i)
    else:
        lax.fori_loop(0, count, lambda i, c: (body(i), c)[1], 0)


def kernel(
    tiles,
    zones,
    image_hbm,
    row_bank_hbm,
    row_index_hbm,
    row_pick_hbm,
    row_mask_hbm,
    column_bank_hbm,
    column_index_hbm,
    column_pick_hbm,
    column_mask_hbm,
    out_hbm,
    image,
    row_bank,
    row_index,
    row_pick,
    row_mask,
    column_bank,
    column_index,
    column_pick,
    column_mask,
    stage,
    held,
    panels,
    arrived,
    out,
    load_sem,
    image_sem,
    send_sem,
    recv_sem,
    edge_send_sem,
    edge_recv_sem,
    store_sem,
):
    me = lax.axis_index("tile")
    zone = lax.axis_index("zone")
    sample_blocks, channels, lines, _ = image.shape
    pieces, piece, _ = stage.shape[1:]
    bank = row_bank_hbm.shape[0]
    bands = row_index.shape[0]
    own_blocks = row_index.shape[2] // tiles
    width = own_blocks * BLOCK
    line_blocks = column_index.shape[1]
    rows = line_blocks * BLOCK

    loads = [
        pltpu.make_async_copy(source, target, load_sem.at[i])
        for i, (source, target) in enumerate(
            (
                (row_index_hbm, row_index),
                (row_pick_hbm, row_pick),
                (row_mask_hbm, row_mask),
                (row_bank_hbm, row_bank.at[pl.ds(0, bank)]),
                (column_index_hbm, column_index),
                (column_pick_hbm, column_pick),
                (column_mask_hbm, column_mask),
                (column_bank_hbm, column_bank.at[pl.ds(0, bank)]),
            )
        )
    ]

    def image_load(i):
        start = i * BLOCK if isinstance(i, int) else pl.multiple_of(i * BLOCK, BLOCK)
        return pltpu.make_async_copy(
            image_hbm.at[0, :, :, pl.ds(start, BLOCK)], image.at[i], image_sem.at[i]
        )

    for load in loads[:3]:
        load.start()
    repeat(sample_blocks, lambda i: image_load(i).start())
    for load in loads[3:]:
        load.start()

    barrier = pltpu.get_barrier_semaphore()

    def greet(i):
        pl.semaphore_signal(
            barrier, inc=1, device_id={"tile": lax.rem(me + i + 1, tiles)}, device_id_type=MESH
        )

    repeat(tiles - 1, greet)

    @pl.when(zone > 0)
    def _():
        pl.semaphore_signal(barrier, inc=1, device_id={"zone": zone - 1}, device_id_type=MESH)

    @pl.when(zone < zones - 1)
    def _():
        pl.semaphore_signal(barrier, inc=1, device_id={"zone": zone + 1}, device_id_type=MESH)

    zero = jnp.zeros((BLOCK, BLOCK), jnp.bfloat16)
    row_bank[bank] = zero
    column_bank[bank] = zero

    for load in loads[:4]:
        load.wait()
    repeat(sample_blocks, lambda i: image_load(i).wait())

    def resampled(column_block):
        parts, kernels = [], []
        for b in range(bands):
            part = image[row_index[b, 0, column_block]]
            parts.append(part.reshape(channels * lines, BLOCK))
            valid = row_mask[b, 0, column_block]
            kernels.append(row_bank[valid * row_pick[b, 0, column_block] + (1 - valid) * bank])
        product = jnp.dot(
            jnp.concatenate(parts, axis=1),
            jnp.concatenate(kernels, axis=0),
            preferred_element_type=jnp.float32,
        )
        return product.astype(jnp.bfloat16)

    def fill(target, tile):
        for j in range(own_blocks):
            block = resampled(tile * own_blocks + j)
            for c in range(channels):
                for p in range(pieces):
                    first = c * lines + p * piece
                    target[p, :, c * width + j * BLOCK : c * width + (j + 1) * BLOCK] = block[
                        first : first + piece
                    ]

    my_lines = pl.ds(me * pieces, pieces)

    def passage(slot, tile):
        return pltpu.make_async_remote_copy(
            src_ref=stage.at[slot],
            dst_ref=held.at[my_lines],
            send_sem=send_sem.at[slot],
            recv_sem=recv_sem.at[me],
            device_id={"tile": tile},
            device_id_type=MESH,
        )

    def offset(i):
        step = tiles // 2 + i
        return jnp.where(step >= tiles, step - tiles + 1, step) if not isinstance(step, int) else (
            step - tiles + 1 if step >= tiles else step
        )

    def send(i):
        tile = lax.rem(me + offset(i), tiles)
        fill(stage.at[i], tile)
        if isinstance(i, int) and i == 0:
            await_greetings()
        passage(i, tile).start()

    def await_greetings():
        @pl.when(zone == 0)
        def _():
            pl.semaphore_wait(barrier, tiles - 1 + (zones > 1))

        @pl.when(zone > 0)
        def _():
            @pl.when(zone < zones - 1)
            def _():
                pl.semaphore_wait(barrier, tiles + 1)

            @pl.when(zone == zones - 1)
            def _():
                pl.semaphore_wait(barrier, tiles)

    if tiles - 1 > 8:
        await_greetings()
    repeat(tiles - 1, send)
    fill(held.at[my_lines], me)

    for load in loads[4:]:
        load.wait()

    def arrival(i):
        tile = lax.rem(me + i + 1, tiles)
        theirs = pl.ds(tile * pieces, pieces)
        pltpu.make_async_remote_copy(
            src_ref=stage.at[i],
            dst_ref=held.at[theirs],
            send_sem=send_sem.at[i],
            recv_sem=recv_sem.at[tile],
            device_id={"tile": tile},
            device_id_type=MESH,
        ).wait_recv()

    repeat(tiles - 1, arrival)

    def gridded(r):
        parts, kernels = [], []
        for b in range(bands):
            for p in range(BLOCK // piece):
                parts.append(held[column_index[0, r, b] * (BLOCK // piece) + p])
            valid = column_mask[0, r, b]
            kernels.append(column_bank[valid * column_pick[0, r, b] + (1 - valid) * bank])
        product = jnp.dot(
            jnp.concatenate(kernels, axis=1),
            jnp.concatenate(parts, axis=0),
            preferred_element_type=jnp.float32,
        )
        return product.astype(jnp.bfloat16)

    def keep(block, row, row_count, first):
        for c in range(channels):
            out[0, c, pl.ds(first, row_count), :] = block[
                row : row + row_count, c * width : (c + 1) * width
            ]

    def handover(side, neighbour):
        return pltpu.make_async_remote_copy(
            src_ref=panels.at[side],
            dst_ref=arrived.at[side],
            send_sem=edge_send_sem.at[side],
            recv_sem=edge_recv_sem.at[side],
            device_id={"zone": neighbour},
            device_id_type=MESH,
        )

    top_to = zone - 1
    bottom_to = zone + 1
    last = line_blocks - 1
    block = gridded(0)
    panels[0] = block[:EDGE]

    @pl.when(zone > 0)
    def _():
        handover(0, top_to).start()

    if last > 0:
        keep(block, EDGE, BLOCK - EDGE, EDGE)
        block = gridded(last)
    panels[1] = block[BLOCK - EDGE :]

    @pl.when(zone < zones - 1)
    def _():
        handover(1, bottom_to).start()

    if last > 0:
        keep(block, 0, BLOCK - EDGE, last * BLOCK)
    if last > 1:

        def middle(i):
            keep(gridded(i + 1), 0, BLOCK, pl.multiple_of((i + 1) * BLOCK, BLOCK))

        repeat(last - 1, middle)

    def stored(i, first, count):
        return pltpu.make_async_copy(
            out.at[:, :, pl.ds(first, count), :],
            out_hbm.at[:, :, pl.ds(first, count), :],
            store_sem.at[i],
        )

    inner = stored(2, EDGE, rows - 2 * EDGE)
    if rows > 2 * EDGE:
        inner.start()
    feather = (
        lax.broadcasted_iota(jnp.int32, (EDGE, channels * width), 0).astype(jnp.float32) + 0.5
    ) / EDGE

    def blend(lower, upper):
        return (
            (1.0 - feather) * lower.astype(jnp.float32) + feather * upper.astype(jnp.float32)
        ).astype(jnp.bfloat16)

    @pl.when(zone > 0)
    def _():
        handover(1, top_to).wait_recv()
        keep(blend(arrived[1], panels[0]), 0, EDGE, 0)

    @pl.when(zone == 0)
    def _():
        keep(panels[0], 0, EDGE, 0)

    top_store = stored(0, 0, EDGE)
    top_store.start()

    @pl.when(zone < zones - 1)
    def _():
        handover(0, bottom_to).wait_recv()
        keep(blend(panels[1], arrived[0]), 0, EDGE, rows - EDGE)

    @pl.when(zone == zones - 1)
    def _():
        keep(panels[1], 0, EDGE, rows - EDGE)

    bottom_store = stored(1, rows - EDGE, EDGE)
    bottom_store.start()

    def sent(i):
        passage(i, lax.rem(me + i + 1, tiles)).wait_send()

    repeat(tiles - 1, sent)

    @pl.when(zone > 0)
    def _():
        handover(0, top_to).wait_send()

    @pl.when(zone < zones - 1)
    def _():
        handover(1, bottom_to).wait_send()

    if rows > 2 * EDGE:
        inner.wait()
    top_store.wait()
    bottom_store.wait()


def solution(mesh):
    tiles = mesh.shape["tile"]
    zones = mesh.shape["zone"]

    def on_device(
        backscatter,
        row_bank,
        row_index,
        row_pick,
        row_mask,
        column_bank,
        column_index,
        column_pick,
        column_mask,
    ):
        _, channels, lines, samples = backscatter.shape
        bank = row_bank.shape[0]
        width = samples // tiles
        piece = min(lines, BLOCK)
        rows = column_index.shape[1] * BLOCK
        row_index, row_pick, row_mask = (
            jnp.transpose(table, (2, 0, 1)) for table in (row_index, row_pick, row_mask)
        )
        dma = pltpu.SemaphoreType.DMA
        return pl.pallas_call(
            functools.partial(kernel, tiles, zones),
            out_shape=jax.ShapeDtypeStruct((1, channels, rows, width), jnp.bfloat16),
            in_specs=[pl.BlockSpec(memory_space=pltpu.HBM)] * 9,
            out_specs=pl.BlockSpec(memory_space=pl.ANY),
            scratch_shapes=[
                pltpu.VMEM((samples // BLOCK, channels, lines, BLOCK), jnp.bfloat16),
                pltpu.VMEM((bank + 1, BLOCK, BLOCK), jnp.bfloat16),
                pltpu.SMEM(row_index.shape, jnp.int32),
                pltpu.SMEM(row_index.shape, jnp.int32),
                pltpu.SMEM(row_index.shape, jnp.int32),
                pltpu.VMEM((bank + 1, BLOCK, BLOCK), jnp.bfloat16),
                pltpu.SMEM(column_index.shape, jnp.int32),
                pltpu.SMEM(column_index.shape, jnp.int32),
                pltpu.SMEM(column_index.shape, jnp.int32),
                pltpu.VMEM((tiles - 1, lines // piece, piece, channels * width), jnp.bfloat16),
                pltpu.VMEM((tiles * lines // piece, piece, channels * width), jnp.bfloat16),
                pltpu.VMEM((2, EDGE, channels * width), jnp.bfloat16),
                pltpu.VMEM((2, EDGE, channels * width), jnp.bfloat16),
                pltpu.VMEM((1, channels, rows, width), jnp.bfloat16),
                dma((8,)),
                dma((samples // BLOCK,)),
                dma((tiles - 1,)),
                dma((tiles,)),
                dma((2,)),
                dma((2,)),
                dma((3,)),
            ],
            compiler_params=pltpu.CompilerParams(
                collective_id=0, has_side_effects=True, vmem_limit_bytes=48 * 2**20
            ),
        )(
            *(
                pltpu.with_memory_space_constraint(operand, pltpu.HBM)
                for operand in (
                    backscatter,
                    row_bank,
                    row_index,
                    row_pick,
                    row_mask,
                    column_bank,
                    column_index,
                    column_pick,
                    column_mask,
                )
            )
        )

    tables = P(("groups", "zone"), None, None)
    return jax.shard_map(
        on_device,
        mesh=mesh,
        in_specs=(
            P(("groups", "zone"), None, "tile", None),
            P(),
            tables,
            tables,
            tables,
            P(),
            tables,
            tables,
            tables,
        ),
        out_specs=P(("groups", "zone"), None, None, "tile"),
        check_vma=False,
    )
```

time: 29.5 us -> 13.1 us (0.44); the launches traced: 29 us -> 13 us
  Pallas kernels: 0 us -> 12.3 us
  starting transfers between devices: 12.3 us -> 0 us
  local copies, waits for them, and re-layouts: 11.8 us -> 0.66 us
  waiting for transfers between devices: 3.26 us -> 0 us
  other arithmetic: 0.91 us -> 0 us
  matrix products: 0.57 us -> 0 us
    pallas_call x0 -> x1, Pallas kernels: none -> 12.3 us  [on_device(): pl.pallas_call(functools.partial(kernel, tiles, zones), out_shape=jax.Sha...]
    ppermute x2 -> x0, starting transfers between devices: 6.83 us -> none  [passed_along(): return lax.ppermute(block, axis, route)]
    all_to_all x1 -> x0, starting transfers between devices: 5.42 us -> none  [on_device(): lax.all_to_all(along_samples, 'tile', split_axis=2, concat_axis=1, tiled=...]
    gather x6 -> x0, local copies, waits for them, and re-layouts: 4.63 us -> none  [the longest x1 1.62 us: on_device(): column_bank[column_pick[0]]]
    unnamed x16 -> x1, local copies, waits for them, and re-layouts: 5.14 us -> 0.66 us
    ppermute x2 -> x0, waiting for transfers between devices: 3.26 us -> none  [passed_along(): return lax.ppermute(block, axis, route)]
    another operation x2 -> x0, local copies, waits for them, and re-layouts: 1.02 us -> none  [on_device(): blocks = image.reshape(channels, lin_dev, column_blocks, BLOCK)]
    broadcast_in_dim x1 -> x0, other arithmetic: 0.67 us -> none  [on_device(): return gridded[None]]
  transfers between devices with their start and end apart: 3 -> 0, of which waited for: 1 -> 0; matrix products, arithmetic and copies ran while one was open for 11% -> 0% of each run, Pallas kernels for 0% -> 0%
where the time goes in v1:
time: 13.1 us; the launch traced here: 13 us
  Pallas kernels  12.3 us (94%)
  local copies, waits for them, and re-layouts  0.66 us (5%)
    pallas_call x1, Pallas kernels, on_device(): pl.pallas_call(functools.partial(kernel, tiles, zones), out_shape=jax.Sha...  12.3 us
    unnamed x1, local copies, waits for them, and re-layouts  0.66 us

profile of v1, /device:TPU:1, one launch (start us, length us, event | category | flops | bytes accessed | tf_op | source)
XLA Modules:
  0.0 13.0 jit_solution(8036681516901552266)
XLA Ops:
  0.0 12.3 %shard_map.91 = bf16[1,2,256,128]{3,2,1,0:T(8,128)(2,1)S(1)} custom-call(bf16[1,2,64,512]{3,2,1,0:T(8,128)(2,1)} %image_hbm.1, bf16[16,128,128]{2,1,0:T(8,128)(2,1)} %row_bank_hbm.1, s32[3,1,4]{2,1,0:T(1,128)} %bitcast.3, s32[3,1,4]{2,1,0:T(1,128)} %bitcast.4, s32[3,1,4]{2,1,0:T(1,128)} %bitcast.5, bf16[16,128,128]{2,1,0:T(8,128)(2,1)} %column_bank_hbm.1, ...), custom_call_target="tpu_custom_call" | custom-call | tf_op jit(solution)/shard_map/pallas_call | solution.py:352
  12.3 0.7 %copy.11 = bf16[1,2,256,128]{3,2,1,0:T(8,128)(2,1)} copy(bf16[1,2,256,128]{3,2,1,0:T(8,128)(2,1)S(1)} %shard_map.91) | data formatting | bytes 262144
